TPU v7x, 32 devices: a whole 2x2x4 slice. The times are simulated.
32 devices in a mesh: dp: 4 (over x, core), expert: 8 (over z, y).
Axes of the slice: x: 2, y: 2, z: 4, core: 2. Of those that a mesh axis runs over, the one named last changes fastest.
Arguments:
- tokens: bfloat16 [1024, 2048], P('expert', 'dp'), may hold values from -6 to 6
- cotangent: bfloat16 [1024, 2048], P('expert', 'dp'), may hold values from -6 to 6
- route: int32 [1024, 8], P('expert'), may hold values from 0 to 23, all different within a row; in each aligned block of 128 rows (0 to 127, 128 to 255, ...) at most 44 rows name the same one
- gate_prob: float32 [1024, 8], P('expert'), may hold values from 0.02 to 0.25
- replica_pick: int32 [8], replicated, may hold values from 0 to 1
- w_gate: bfloat16 [16, 1536, 2048], P('expert', 'dp'), may hold values from -0.125 to 0.125
- w_up: bfloat16 [16, 1536, 2048], P('expert', 'dp'), may hold values from -0.125 to 0.125
- w_down: bfloat16 [16, 1536, 2048], P('expert', 'dp'), may hold values from -0.15625 to 0.15625
Outputs:
- layer_out: bfloat16 [1024, 2048], P('expert', 'dp')
- token_grad: bfloat16 [1024, 2048], P('expert', 'dp')
- gate_grad: float32 [1024, 8], P('expert', 'dp')
- w_gate_grad: bfloat16 [16, 1536, 2048], P('expert', 'dp')
- w_up_grad: bfloat16 [16, 1536, 2048], P('expert', 'dp')
- w_down_grad: bfloat16 [16, 1536, 2048], P('expert', 'dp')
Inputs may be any that keep to these rules, and one draw needn't show every extreme that they name: `route`: each row names 8 different copies. Among the rows of one device, in aligned blocks of 128 tokens, no copy is named more than 44 times, a bound that some block reaches.
All inputs are finite; a program needn't handle non-finite values.
Results may differ from a plain program's by a relative error of at most 0.014.
Values may be sent and summed in bfloat16 or wider, within the bound.
A program may use at most 128 MiB of HBM per device.

v0:
```python
import functools
import itertools
import math

import jax
import jax.numpy as jnp
from jax import lax
from jax.experimental import pallas as pl
from jax.experimental.pallas import tpu as pltpu
from jax.sharding import PartitionSpec as P

MESH = pl.DeviceIdType.MESH
GATHER_ORDERS = ((0, 1, 2, 3), (0, 2, 1, 3))
REDUCE_ORDERS = ((3, 2, 1, 0), (3, 1, 2, 0))


def lines():
    experts, dps = lax.axis_size("expert"), lax.axis_size("dp")
    along_y = math.isqrt(experts // 2)
    return (experts // along_y, along_y, dps // 2, 2)


def flipped(index, bits):
    result, bit = index, 1
    while bit <= bits:
        if bits & bit:
            result = result + bit - 2 * bit * lax.rem(lax.div(index, bit), 2)
        bit *= 2
    return result


class Place:
    def __init__(self, sizes):
        self.sizes = sizes
        self.expert, self.dp = lax.axis_index("expert"), lax.axis_index("dp")
        self.ids = list(itertools.product(*[range(s) for s in sizes]))

    def expert_of(self, d):
        return flipped(self.expert, d[0] * self.sizes[1] + d[1])

    def dp_of(self, d):
        return flipped(self.dp, d[2] * self.sizes[3] + d[3])

    def device(self, d):
        return {"dp": self.dp_of(d), "expert": self.expert_of(d)}

    def number(self, d):
        z, y, x, c = self.sizes
        return ((d[0] * y + d[1]) * x + d[2]) * c + d[3]

    def steps(self, dim):
        out = []
        for delta in range(1, self.sizes[dim]):
            step = [0, 0, 0, 0]
            step[dim] = delta
            out.append(tuple(step))
        return out

    def block(self, ref, d, rows, columns):
        return ref.at[
            pl.ds(pl.multiple_of(self.expert_of(d) * rows, rows), rows),
            pl.ds(pl.multiple_of(self.dp_of(d) * columns, columns), columns),
        ]

    def greet(self):
        barrier = pltpu.get_barrier_semaphore()
        peers = [s for dim in range(4) for s in self.steps(dim)]
        for peer in peers:
            pl.semaphore_signal(barrier, inc=1, device_id=self.device(peer), device_id_type=MESH)
        pl.semaphore_wait(barrier, len(peers))


def plus(a, b):
    return tuple(i ^ j for i, j in zip(a, b))


def remote(src, dst, send, recv, device):
    return pltpu.make_async_remote_copy(
        src_ref=src, dst_ref=dst, send_sem=send, recv_sem=recv, device_id=device, device_id_type=MESH
    )


def gather_kernel(sizes, tok_ref, cot_ref, meta_ref, tok_out, cot_out, meta_out, send, recv, own):
    place = Place(sizes)
    rows, columns = tok_ref.shape

    def view(a, ref, d):
        if a == 2:
            return ref.at[place.expert_of(d)]
        return place.block(ref, d, rows, columns)

    ins, outs = (tok_ref, cot_ref, meta_ref), (tok_out, cot_out, meta_out)
    orders = GATHER_ORDERS + ((0, 1),)
    zero = (0, 0, 0, 0)
    local = [pltpu.make_async_copy(ins[a], view(a, outs[a], zero), own.at[a]) for a in range(3)]
    for copy in local:
        copy.start()
    place.greet()
    sent = []

    def stage_of(a, d):
        return max([p for p, dim in enumerate(orders[a]) if d[dim]], default=-1)

    def forward(a, d, p):
        for step in place.steps(orders[a][p]):
            there = plus(d, step)
            n = place.number(there)
            src = ins[a] if d == zero else view(a, outs[a], d)
            copy = remote(src, view(a, outs[a], d), send.at[a, n], recv.at[a, n], place.device(step))
            copy.start()
            sent.append(copy)

    for p in range(4):
        for a in (2, 0, 1):
            if p < len(orders[a]):
                forward(a, zero, p)
    for stage in range(4):
        todo = []
        for a in (2, 0, 1):
            if stage < len(orders[a]):
                mine = [d for d in place.ids if all(d[x] == 0 for x in range(4) if x not in orders[a])]
                todo += [(i, a, d) for i, d in enumerate([d for d in mine if stage_of(a, d) == stage])]
        for _, a, d in sorted(todo, key=lambda t: t[0]):
            n = place.number(d)
            here = view(a, outs[a], d)
            remote(here, here, send.at[a, n], recv.at[a, n], place.device(place.steps(0)[0])).wait_recv()
            for p in range(stage + 1, len(orders[a])):
                forward(a, d, p)
    for copy in local:
        copy.wait()
    for copy in sent:
        copy.wait_send()


def gather_all(tokens, cotangent, meta):
    sizes = lines()
    groups, dps = lax.axis_size("expert"), lax.axis_size("dp")
    devices = groups * dps
    whole = jax.ShapeDtypeStruct((groups * tokens.shape[0], dps * tokens.shape[1]), jnp.bfloat16)
    return pl.pallas_call(
        functools.partial(gather_kernel, sizes),
        out_shape=(whole, whole, jax.ShapeDtypeStruct((groups,) + meta.shape, meta.dtype)),
        in_specs=[pl.BlockSpec(memory_space=pl.ANY)] * 3,
        out_specs=[pl.BlockSpec(memory_space=pl.ANY)] * 3,
        scratch_shapes=[
            pltpu.SemaphoreType.DMA((3, devices)),
            pltpu.SemaphoreType.DMA((3, devices)),
            pltpu.SemaphoreType.DMA((3,)),
        ],
        compiler_params=pltpu.CompilerParams(collective_id=0, has_side_effects=True),
        name="gather_all",
    )(tokens, cotangent, meta)


def reduce_kernel(sizes, out_ref, back_ref, gg_ref, layer_ref, grad_ref, prob_ref, stage, slots, gg_stage, gg_slots, send, recv, own, gg_send, gg_recv):
    place = Place(sizes)
    z_size, y_size, x_size, _ = sizes
    _, _, rows, columns = slots.shape
    refs, results = (out_ref, back_ref), (layer_ref, grad_ref)
    zero = (0, 0, 0, 0)
    kept = [d for d in place.ids if d[3] == 0]
    local = {}
    for a in range(2):
        for d in kept:
            n = place.number(d) // 2
            local[a, d] = pltpu.make_async_copy(place.block(refs[a], d, rows, columns), stage.at[a, n], own.at[a, n])
            local[a, d].start()
    place.greet()
    sent = []

    def first(a, d):
        return min([p for p, dim in enumerate(REDUCE_ORDERS[a]) if d[dim]], default=4)

    def push(a, d, p):
        dim = REDUCE_ORDERS[a][p]
        step = tuple(d[i] if i == dim else 0 for i in range(4))
        n = place.number(d)
        src = place.block(refs[a], d, rows, columns) if p == 0 else stage.at[a, n // 2]
        copy = remote(src, slots.at[a, n], send.at[a, n], recv.at[a, n], place.device(step))
        copy.start()
        sent.append(copy)

    def total(a, d, p):
        local[a, d].wait()
        value = stage[a, place.number(d) // 2].astype(jnp.float32)
        for q in range(p):
            for step in place.steps(REDUCE_ORDERS[a][q]):
                n = place.number(plus(d, step))
                remote(slots.at[a, n], slots.at[a, n], send.at[a, n], recv.at[a, n], place.device(place.steps(0)[0])).wait_recv()
                value = value + slots[a, n].astype(jnp.float32)
        return value.astype(jnp.bfloat16)

    def gg_push(src, n, step):
        copy = remote(src, gg_slots.at[n], gg_send.at[n], gg_recv.at[n], place.device(step))
        copy.start()
        sent.append(copy)

    def gg_take(n):
        remote(gg_slots.at[n], gg_slots.at[n], gg_send.at[n], gg_recv.at[n], place.device(place.steps(0)[0])).wait_recv()
        return gg_slots[n]

    experts = z_size * y_size

    def gg_step(p):
        if p == 0:
            for dz in range(z_size):
                for dy in range(1, y_size):
                    d = (dz, dy, 0, 0)
                    gg_push(gg_ref.at[place.expert_of(d)], dz * y_size + dy, (0, dy, 0, 0))
        elif p == 1:
            for dz in range(z_size):
                value = gg_ref[place.expert_of((dz, 0, 0, 0))]
                for dy in range(1, y_size):
                    value = value + gg_take(dz * y_size + dy)
                gg_stage[dz] = value
                if dz:
                    gg_push(gg_stage.at[dz], dz * y_size, (dz, 0, 0, 0))
        elif p == 2:
            value = gg_stage[0]
            for dz in range(1, z_size):
                value = value + gg_take(dz * y_size)
            gg_stage[z_size] = value
            for dx in range(1, x_size):
                gg_push(gg_stage.at[z_size], experts + dx, (0, 0, dx, 0))
        elif p == 3:
            value = gg_stage[z_size]
            for dx in range(1, x_size):
                value = value + gg_take(experts + dx)
            gg_stage[z_size + 1] = value
            gg_push(gg_stage.at[z_size + 1], experts + x_size, (0, 0, 0, 1))
        else:
            prob_ref[...] = gg_stage[z_size + 1] + gg_take(experts + x_size)

    for p in range(5):
        todo = []
        for a in range(2):
            mine = [d for d in place.ids if first(a, d) == p]
            mine.sort(key=lambda d: [d[dim] == 0 for dim in REDUCE_ORDERS[a]])
            todo += [(i, a, d) for i, d in enumerate(mine)]
        for _, a, d in sorted(todo, key=lambda t: t[0]):
            if p == 4:
                results[a][...] = total(a, d, p)
            else:
                if p:
                    stage[a, place.number(d) // 2] = total(a, d, p)
                push(a, d, p)
        gg_step(p)
    for copy in sent:
        copy.wait_send()


def reduce_all(out_tok, back_tok, gg, rows, columns):
    sizes = lines()
    devices = sizes[0] * sizes[1] * sizes[2] * sizes[3]
    block = jax.ShapeDtypeStruct((rows, columns), jnp.bfloat16)
    vmem = pl.BlockSpec(memory_space=pltpu.VMEM)
    few = sizes[0] * sizes[1] + sizes[2] + 1
    return pl.pallas_call(
        functools.partial(reduce_kernel, sizes),
        out_shape=(block, block, jax.ShapeDtypeStruct(gg.shape[1:], gg.dtype)),
        in_specs=[pl.BlockSpec(memory_space=pl.ANY)] * 2 + [vmem],
        out_specs=[vmem] * 3,
        scratch_shapes=[
            pltpu.VMEM((2, devices // 2, rows, columns), jnp.bfloat16),
            pltpu.VMEM((2, devices, rows, columns), jnp.bfloat16),
            pltpu.VMEM((sizes[0] + 2,) + gg.shape[1:], gg.dtype),
            pltpu.VMEM((few,) + gg.shape[1:], gg.dtype),
            pltpu.SemaphoreType.DMA((2, devices)),
            pltpu.SemaphoreType.DMA((2, devices)),
            pltpu.SemaphoreType.DMA((2, devices // 2)),
            pltpu.SemaphoreType.DMA((few,)),
            pltpu.SemaphoreType.DMA((few,)),
        ],
        compiler_params=pltpu.CompilerParams(
            collective_id=1, has_side_effects=True, vmem_limit_bytes=54 * 1024 * 1024
        ),
        name="reduce_all",
    )(out_tok, back_tok, gg)


def finish_kernel(
    sizes, hid_ref, dg_ref, du_ref, sel_ref, pt_ref, gg_ref, rin_ref, rcot_ref, wg_ref, wu_ref, wd_ref, cg_ref, cu_ref, cd_ref,
    layer_ref, grad_ref, prob_ref, wgg_ref, wug_ref, wdg_ref,
    stage, slots, wide, rows_buf, made, tiles, gg_stage, gg_slots, send, recv, loaded, stored, gg_send, gg_recv,
):
    place = Place(sizes)
    z_size, y_size, x_size, _ = sizes
    _, _, rows, columns = slots.shape
    results = (layer_ref, grad_ref)
    owned = wg_ref.shape[0]
    slot_rows = hid_ref.shape[1]
    tokens = pt_ref.shape[0]
    f32, bf16 = jnp.float32, jnp.bfloat16

    loads = []
    for i, (own, guest) in enumerate(((wd_ref, cd_ref), (wg_ref, cg_ref), (wu_ref, cu_ref))):
        loads.append(pltpu.make_async_copy(own, wide.at[i, pl.ds(0, owned)], loaded.at[2 * i]))
        loads.append(pltpu.make_async_copy(guest, wide.at[i, pl.ds(owned, 1)], loaded.at[2 * i + 1]))
    loads.append(pltpu.make_async_copy(rin_ref, rows_buf.at[0], loaded.at[6]))
    loads.append(pltpu.make_async_copy(rcot_ref, rows_buf.at[1], loaded.at[7]))
    for copy in loads:
        copy.start()
    barrier = pltpu.get_barrier_semaphore()
    peers = [s for dim in range(4) for s in place.steps(dim)]
    for peer in peers:
        pl.semaphore_signal(barrier, inc=1, device_id=place.device(peer), device_id_type=MESH)
    sent = []

    def granule(a, d):
        return stage.at[a, d[2] * 2 + d[3], pl.ds(pl.multiple_of(place.expert_of(d) * rows, rows), rows)]

    def first(a, d):
        return min([p for p, dim in enumerate(REDUCE_ORDERS[a]) if d[dim]], default=4)

    def make(a, d):
        cols = pl.ds(pl.multiple_of(place.dp_of(d) * columns, columns), columns)
        for c in range(owned + 1):
            if a == 0:
                part = jnp.dot(hid_ref[c], wide[0, c, :, cols], preferred_element_type=f32)
            else:
                part = jnp.dot(dg_ref[c], wide[1, c, :, cols], preferred_element_type=f32)
                part = part + jnp.dot(du_ref[c], wide[2, c, :, cols], preferred_element_type=f32)
            made[pl.ds(c * slot_rows, slot_rows)] = part.astype(bf16)
        step = 2 * rows

        @pl.loop(0, tokens // step)
        def _(i):
            at = pl.ds(pl.multiple_of(i * step, step), step)
            sums = jnp.dot(pt_ref[at], made[...], preferred_element_type=f32)
            stage[a, d[2] * 2 + d[3], at] = sums.astype(bf16)

    def push(a, d, p):
        dim = REDUCE_ORDERS[a][p]
        step = tuple(d[i] if i == dim else 0 for i in range(4))
        n = place.number(d)
        copy = remote(granule(a, d), slots.at[a, n], send.at[a, n], recv.at[a, n], place.device(step))
        copy.start()
        sent.append(copy)

    def total(a, d, p):
        value = granule(a, d)[...].astype(f32)
        for q in range(p):
            for step in place.steps(REDUCE_ORDERS[a][q]):
                n = place.number(plus(d, step))
                remote(slots.at[a, n], slots.at[a, n], send.at[a, n], recv.at[a, n], place.device(place.steps(0)[0])).wait_recv()
                value = value + slots[a, n].astype(f32)
        return value.astype(bf16)

    def gg_push(src, n, step):
        copy = remote(src, gg_slots.at[n], gg_send.at[n], gg_recv.at[n], place.device(step))
        copy.start()
        sent.append(copy)

    def gg_take(n):
        remote(gg_slots.at[n], gg_slots.at[n], gg_send.at[n], gg_recv.at[n], place.device(place.steps(0)[0])).wait_recv()
        return gg_slots[n]

    experts = z_size * y_size

    def gg_step(p):
        if p == 0:
            for dz in range(z_size):
                for dy in range(1, y_size):
                    d = (dz, dy, 0, 0)
                    gg_push(gg_ref.at[place.expert_of(d)], dz * y_size + dy, (0, dy, 0, 0))
        elif p == 1:
            for dz in range(z_size):
                value = gg_ref[place.expert_of((dz, 0, 0, 0))]
                for dy in range(1, y_size):
                    value = value + gg_take(dz * y_size + dy)
                gg_stage[dz] = value
                if dz:
                    gg_push(gg_stage.at[dz], dz * y_size, (dz, 0, 0, 0))
        elif p == 2:
            value = gg_stage[0]
            for dz in range(1, z_size):
                value = value + gg_take(dz * y_size)
            gg_stage[z_size] = value
            for dx in range(1, x_size):
                gg_push(gg_stage.at[z_size], experts + dx, (0, 0, dx, 0))
        elif p == 3:
            value = gg_stage[z_size]
            for dx in range(1, x_size):
                value = value + gg_take(experts + dx)
            gg_stage[z_size + 1] = value
            gg_push(gg_stage.at[z_size + 1], experts + x_size, (0, 0, 0, 1))
        else:
            prob_ref[...] = gg_stage[z_size + 1] + gg_take(experts + x_size)

    lefts, outs = (hid_ref, dg_ref, du_ref), (wdg_ref, wgg_ref, wug_ref)
    stores = []

    def weight_grad(task):
        w, j = divmod(task, owned)
        if task == 0:
            loads[6].wait()
            loads[7].wait()
        if task >= 2:
            stores[task - 2].wait()
        slot, right = task % 2, 1 if w == 0 else 0
        step = 512

        @pl.loop(0, wide.shape[3] // step)
        def _(i):
            at = pl.ds(pl.multiple_of(i * step, step), step)
            dims = (((0,), (0,)), ((), ()))
            value = lax.dot_general(lefts[w][j], rows_buf[right, j, :, at], dims, preferred_element_type=f32)
            value = value + lax.dot_general(sel_ref[w, j], rows_buf[right, owned, :, at], dims, preferred_element_type=f32)
            tiles[slot, :, at] = value.astype(bf16)

        copy = pltpu.make_async_copy(tiles.at[slot], outs[w].at[j], stored.at[task])
        copy.start()
        stores.append(copy)

    waited = False
    slices = sorted({d[2:] for d in place.ids}, key=lambda s: (s[1] == 0, s[0] == 0))
    for s in slices:
        for a in range(2):
            if s == slices[0]:
                for copy in loads[:2] if a == 0 else loads[2:6]:
                    copy.wait()
            make(a, (0, 0) + s)
            if not waited:
                pl.semaphore_wait(barrier, len(peers))
                waited = True
                gg_step(0)
            if s[1]:
                mine = [d for d in place.ids if d[2:] == s]
                mine.sort(key=lambda d: [d[dim] == 0 for dim in REDUCE_ORDERS[a]])
                for d in mine:
                    push(a, d, 0)
            elif a == 0 and s[0]:
                for d in place.ids:
                    if d[2:] == s:
                        n = granule(a, d)
                        n[...] = total(a, d, 1)
                        push(a, d, 1)
    tasks = 3 * owned
    spread = {1: range(0, tasks // 2), 2: range(tasks // 2, tasks - 1), 3: range(tasks - 1, tasks)}
    for p in range(1, 5):
        todo = []
        for a in range(2):
            mine = [d for d in place.ids if first(a, d) == p and not (p == 1 and a == 0)]
            mine.sort(key=lambda d: [d[dim] == 0 for dim in REDUCE_ORDERS[a]])
            todo += [(i, a, d) for i, d in enumerate(mine)]
        for _, a, d in sorted(todo, key=lambda t: t[0]):
            if p == 4:
                results[a][...] = total(a, d, p)
            else:
                n = granule(a, d)
                n[...] = total(a, d, p)
                push(a, d, p)
        gg_step(p)
        for task in spread.get(p, ()):
            weight_grad(task)
    for copy in stores[-2:]:
        copy.wait()
    for copy in sent:
        copy.wait_send()


def finish(hidden, d_gate, d_up, select, pick_t, gg, rows_in, rows_cot, w_gate, w_up, w_down, chosen, rows, columns):
    sizes = lines()
    devices = sizes[0] * sizes[1] * sizes[2] * sizes[3]
    owned, width, features = w_gate.shape
    sel = jnp.stack([jnp.stack([left[owned] * s for s in select]) for left in (hidden, d_gate, d_up)])
    block = jax.ShapeDtypeStruct((rows, columns), jnp.bfloat16)
    grad = jax.ShapeDtypeStruct(w_gate.shape, jnp.bfloat16)
    vmem, anywhere = pl.BlockSpec(memory_space=pltpu.VMEM), pl.BlockSpec(memory_space=pl.ANY)
    few = sizes[0] * sizes[1] + sizes[2] + 1
    dps = sizes[2] * sizes[3]
    bf16 = jnp.bfloat16
    return pl.pallas_call(
        functools.partial(finish_kernel, sizes),
        out_shape=(block, block, jax.ShapeDtypeStruct(gg.shape[1:], gg.dtype), grad, grad, grad),
        in_specs=[vmem] * 6 + [anywhere] * 8,
        out_specs=[vmem] * 3 + [anywhere] * 3,
        scratch_shapes=[
            pltpu.VMEM((2, dps, pick_t.shape[0], columns), bf16),
            pltpu.VMEM((2, devices, rows, columns), bf16),
            pltpu.VMEM((3, owned + 1, width, features), bf16),
            pltpu.VMEM((2,) + rows_in.shape, bf16),
            pltpu.VMEM((pick_t.shape[1], columns), bf16),
            pltpu.VMEM((2, width, features), bf16),
            pltpu.VMEM((sizes[0] + 2,) + gg.shape[1:], gg.dtype),
            pltpu.VMEM((few,) + gg.shape[1:], gg.dtype),
            pltpu.SemaphoreType.DMA((2, devices)),
            pltpu.SemaphoreType.DMA((2, devices)),
            pltpu.SemaphoreType.DMA((8,)),
            pltpu.SemaphoreType.DMA((3 * owned,)),
            pltpu.SemaphoreType.DMA((few,)),
            pltpu.SemaphoreType.DMA((few,)),
        ],
        compiler_params=pltpu.CompilerParams(
            collective_id=1, has_side_effects=True, vmem_limit_bytes=60 * 1024 * 1024
        ),
        name="finish",
    )(hidden, d_gate, d_up, sel, pick_t, gg, rows_in, rows_cot, w_gate, w_up, w_down, *chosen)


def body(tokens, cotangent, route, gate_prob, replica_pick, w_gate, w_up, w_down):
    groups = lax.axis_size("expert")
    column = lax.axis_index("expert")
    tok_dev, slice_width = tokens.shape
    fanout = route.shape[1]
    owned, width, features = w_gate.shape
    local_copies = owned + 1
    copies = groups * local_copies
    capacity = tok_dev * fanout // copies + 2
    half_axis = groups // 2
    rows = groups * capacity
    total = groups * tok_dev
    f32, bf16 = jnp.float32, jnp.bfloat16

    meta = jnp.concatenate([route.T.astype(f32), gate_prob.T], axis=0)
    tok, cot, meta = gather_all(tokens, cotangent, meta)
    meta = jnp.transpose(meta, (1, 0, 2)).reshape(2 * fanout, total)
    route_t = meta[:fanout].astype(jnp.int32)
    gate_t = meta[fanout:]

    partner = (column + half_axis) % groups
    own_pick = replica_pick[partner]
    select = [(own_pick == j).astype(bf16) for j in range(owned)]
    copy_ids = [column * local_copies + j for j in range(owned)] + [partner * local_copies + owned]

    hits = [route_t == c for c in copy_ids]
    member = jnp.stack([jnp.sum(h.astype(f32), axis=0) for h in hits])
    gate_of = jnp.stack([jnp.sum(jnp.where(h, gate_t, 0.0), axis=0) for h in hits])
    blocks = member.reshape(local_copies, groups, tok_dev)
    tri = (jnp.arange(tok_dev)[:, None] <= jnp.arange(tok_dev)[None, :]).astype(bf16)
    inside = jnp.einsum("cgt,tu->cgu", blocks.astype(bf16), tri, preferred_element_type=f32)
    sums = jnp.sum(blocks, axis=2)
    before = (jnp.arange(groups)[:, None] < jnp.arange(groups)[None, :]).astype(f32)
    offset = jnp.sum(sums[:, :, None] * before[None], axis=1)
    place = (inside + offset[:, :, None]).reshape(local_copies, total) - 1.0
    place = jnp.where(member > 0, place, -1.0).astype(jnp.int32)
    picks = place[:, None, :] == jnp.arange(rows, dtype=jnp.int32)[None, :, None]
    pick = picks.astype(bf16)
    gate_rows = jnp.sum(jnp.where(picks, gate_of[:, None, :], 0.0), axis=2)

    chosen = [lax.dynamic_index_in_dim(w, own_pick, 0, keepdims=True) for w in (w_gate, w_up, w_down)]
    gate_w = jnp.concatenate([w_gate, chosen[0]], axis=0)
    up_w = jnp.concatenate([w_up, chosen[1]], axis=0)
    down_w = jnp.concatenate([w_down, chosen[2]], axis=0)

    rows_in = jnp.einsum("crt,td->crd", pick, tok, preferred_element_type=f32).astype(bf16)
    gate_act = jnp.einsum("crd,cfd->crf", rows_in, gate_w, preferred_element_type=f32)
    up_act = jnp.einsum("crd,cfd->crf", rows_in, up_w, preferred_element_type=f32)
    sig = jax.nn.sigmoid(gate_act)
    activated = gate_act * sig
    hidden = activated * up_act
    g = gate_rows[:, :, None]
    hidden_g = (g * hidden).astype(bf16)

    rows_cot = jnp.einsum("crt,td->crd", pick, cot, preferred_element_type=f32).astype(bf16)
    back_h = jnp.einsum("crd,cfd->crf", rows_cot, down_w, preferred_element_type=f32)
    gg_rows = jnp.sum(hidden * back_h, axis=2)
    d_hidden = g * back_h
    d_gate = (d_hidden * up_act * sig * (1.0 + gate_act * (1.0 - sig))).astype(bf16)
    d_up = (d_hidden * activated).astype(bf16)
    gg_tok = jnp.sum(jnp.where(picks, gg_rows[:, :, None], 0.0), axis=1)
    gg = sum(jnp.where(h, gg_tok[j][None], 0.0) for j, h in enumerate(hits))
    gg = jnp.transpose(gg.reshape(fanout, groups, tok_dev), (1, 0, 2))
    share = fanout // lax.axis_size("dp")
    if 8 * total * features > 1 << 25:
        out_rows = jnp.einsum("crf,cfd->crd", hidden_g, down_w, preferred_element_type=f32).astype(bf16)
        out_tok = jnp.einsum("crt,crd->td", pick, out_rows, preferred_element_type=f32).astype(bf16)
        back_rows = jnp.einsum("crf,cfd->crd", d_gate, gate_w, preferred_element_type=f32)
        back_rows = back_rows + jnp.einsum("crf,cfd->crd", d_up, up_w, preferred_element_type=f32)
        back_tok = jnp.einsum("crt,crd->td", pick, back_rows.astype(bf16), preferred_element_type=f32).astype(bf16)
        layer_out, token_grad, gg = reduce_all(out_tok, back_tok, gg, tok_dev, slice_width)

        def weight_grad(left, right):
            parts = []
            for j in range(owned):
                both_l = jnp.concatenate([left[j], left[owned] * select[j]], axis=0)
                both_r = jnp.concatenate([right[j], right[owned]], axis=0)
                parts.append(jnp.einsum("rf,rd->fd", both_l, both_r, preferred_element_type=f32).astype(bf16))
            return jnp.stack(parts)

        grads = weight_grad(d_gate, rows_in), weight_grad(d_up, rows_in), weight_grad(hidden_g, rows_cot)
    else:
        slot = jnp.where(place < 0, -1, place + rows * jnp.arange(local_copies, dtype=jnp.int32)[:, None]).T
        every = jnp.arange(local_copies * rows, dtype=jnp.int32)[None, :]
        pick_t = sum((slot[:, j : j + 1] == every).astype(bf16) for j in range(local_copies))
        layer_out, token_grad, gg, *grads = finish(
            hidden_g, d_gate, d_up, select, pick_t, gg, rows_in, rows_cot, w_gate, w_up, w_down, chosen, tok_dev, slice_width
        )
    gate_grad = lax.dynamic_slice_in_dim(gg, lax.axis_index("dp") * share, share, 0).T
    return (layer_out, token_grad, gate_grad, *grads)


def solution(mesh):
    in_specs = (
        P("expert", "dp"),
        P("expert", "dp"),
        P("expert", None),
        P("expert", None),
        P(),
        P("expert", "dp", None),
        P("expert", "dp", None),
        P("expert", "dp", None),
    )
    out_specs = (
        P("expert", "dp"),
        P("expert", "dp"),
        P("expert", "dp"),
        P("expert", "dp", None),
        P("expert", "dp", None),
        P("expert", "dp", None),
    )
    return jax.shard_map(body, mesh=mesh, in_specs=in_specs, out_specs=out_specs, check_vma=False)
```

profile of v0, /device:TPU:0, one launch (start us, length us, event | category | flops | bytes accessed | tf_op | source)
XLA Modules:
  0.0 189.3 jit_solution(14120080200131508879)
XLA Ops:
  0.7 1.4 dynamic_slice.16
  5.3 0.7 convert_bitcast_fusion
  6.0 1.3 pad_maximum_fusion.3.meta_ref
  7.3 2.7 %constant_dynamic-slice_fusion.2.cg_ref = bf16[1,384,2048]{2,1,0:T(8,128)(2,1)} fusion(bf16[2,384,2048]{2,1,0:T(8,128)(2,1)} %wg_ref.1, s32[]{:T(128)S(6)} %select_n.72), kind=kLoop, calls=%fused_computation.79 | loop fusion | bytes 3145732 | tf_op jit(solution)/shard_map/jit(dynamic_index_in_dim)/dynamic_slice | solution.py:541
  10.1 3.4 %constant_dynamic-slice_fusion = (bf16[1,384,2048]{2,1,0:T(8,128)(2,1)}, bf16[1,384,2048]{2,1,0:T(8,128)(2,1)}) fusion(bf16[2,384,2048]{2,1,0:T(8,128)(2,1)S(1)} %copy-done, s32[]{:T(128)S(6)} %select_n.72, bf16[2,384,2048]{2,1,0:T(8,128)(2,1)} %wu_ref.1), kind=kLoop, calls=%fused_computation.77 | loop fusion | bytes 6291460 | tf_op jit(solution)/shard_map/jit(dynamic_index_in_dim)/dynamic_slice | solution.py:541
  13.4 51.4 %gather_all.1 = (bf16[1024,2048]{1,0:T(8,128)(2,1)}, bf16[1024,2048]{1,0:T(8,128)(2,1)}, f32[8,16,128]{2,1,0:T(8,128)}) custom-call(bf16[128,512]{1,0:T(8,128)(2,1)} %tok_ref.1, bf16[128,512]{1,0:T(8,128)(2,1)} %cot_ref.1, f32[16,128]{1,0:T(8,128)} %pad_maximum_fusion.3.meta_ref), custom_call_target="tpu_custom_call" | custom-call | tf_op jit(solution)/shard_map/gather_all/pallas_call | solution.py:140
  64.8 0.9 select_reduce_fusion.4
  65.7 0.1 fusion.38
  65.8 0.1 multiply_reduce_fusion.1
  65.9 0.1 fusion.31
  66.0 0.1 select_bitcast_fusion
  66.1 7.2 %fusion.19.rin_ref = bf16[3,352,2048]{2,1,0:T(8,128)(2,1)S(1)} fusion(bf16[1024,2048]{1,0:T(8,128)(2,1)} %get-tuple-element.16, s32[3,1024]{1,0:T(4,128)S(1)} %get-tuple-element.33), kind=kOutput, calls=%fused_computation.25 | convolution fusion | flops 4432429056 | bytes 8531968 | tf_op jit(solution)/shard_map/crt,td->crd/dot_general | solution.py:546
  73.4 5.0 %fusion.22.rcot_ref = bf16[3,352,2048]{2,1,0:T(8,128)(2,1)S(1)} fusion(bf16[1024,2048]{1,0:T(8,128)(2,1)S(1)} %copy-done.13, s32[3,1024]{1,0:T(4,128)S(1)} %get-tuple-element.33), kind=kOutput, calls=%fused_computation.26 | convolution fusion | flops 4432429056 | bytes 8531968 | tf_op jit(solution)/shard_map/crt,td->crd/dot_general | solution.py:555
  78.4 2.4 %fusion.4 = f32[3,352,384]{2,1,0:T(8,128)S(1)} fusion(bf16[3,352,2048]{2,1,0:T(8,128)(2,1)S(1)} %fusion.19.rin_ref, bf16[1,384,2048]{2,1,0:T(8,128)(2,1)S(1)} %copy-done.5, bf16[2,384,2048]{2,1,0:T(8,128)(2,1)S(1)} %copy-done.1), kind=kOutput, calls=%fused_computation.4 | convolution fusion | flops 1663303680 | bytes 10665984 | tf_op jit(solution)/shard_map/crd,cfd->crf/dot_general | solution.py:548
  80.9 1.0 copy-done.2
  81.9 0.5 copy-done.3
  82.3 2.4 %fusion = f32[3,352,384]{2,1,0:T(8,128)S(1)} fusion(bf16[3,352,2048]{2,1,0:T(8,128)(2,1)S(1)} %fusion.19.rin_ref, bf16[1,384,2048]{2,1,0:T(8,128)(2,1)S(1)} %copy-done.3, bf16[2,384,2048]{2,1,0:T(8,128)(2,1)S(1)} %copy-done.2), kind=kOutput, calls=%fused_computation | convolution fusion | flops 1663303680 | bytes 10665984 | tf_op jit(solution)/shard_map/crd,cfd->crf/dot_general | solution.py:547
  84.8 2.6 %multiply_reduce_fusion = (f32[3,352]{1,0:T(4,128)S(1)}, f32[3,352,384]{2,1,0:T(8,128)S(1)}) fusion(f32[3,352,384]{2,1,0:T(8,128)S(1)} %fusion.4, f32[3,352,384]{2,1,0:T(8,128)S(1)} %fusion, bf16[3,352,2048]{2,1,0:T(8,128)(2,1)S(1)} %fusion.22.rcot_ref, bf16[1,384,2048]{2,1,0:T(8,128)(2,1)S(1)} %copy-done.4, bf16[2,384,2048]{2,1,0:T(8,128)(2,1)S(1)} %copy-done), kind=kOutput, calls=%fused_computation.32 | convolution fusion | flops 1666141184 | bytes 13914240 | tf_op jit(solution)/shard_map/crd,cfd->crf/dot_general | solution.py:556
  87.3 1.4 select_reduce_fusion
  88.7 1.0 multiply_convert_fusion
  89.8 0.7 add_bitcast_fusion.gg_ref
  90.6 0.1 maximum_bitcast_fusion.2
  90.9 1.4 pad_maximum_fusion.sel_ref
  92.3 2.9 %fusion.25.pt_ref = bf16[1024,1056]{1,0:T(8,128)(2,1)} fusion(s32[1024]{0:T(1024)S(1)} %bitcast.66, s32[1024]{0:T(1024)S(1)} %bitcast.67, s32[1024]{0:T(1024)S(1)} %bitcast.65), kind=kLoop, calls=%fused_computation.27 | loop fusion | flops 12976128 | bytes 2174976 | tf_op jit(solution)/shard_map/add | solution.py:585
  95.2 80.9 %finish.1 = (bf16[128,512]{1,0:T(8,128)(2,1)}, bf16[128,512]{1,0:T(8,128)(2,1)}, f32[8,128]{1,0:T(8,128)}, bf16[2,384,2048]{2,1,0:T(8,128)(2,1)}, bf16[2,384,204...) custom-call(bf16[3,352,384]{2,1,0:T(8,128)(2,1)} %copy-done.8, bf16[3,352,384]{2,1,0:T(8,128)(2,1)} %copy-done.7, ...), custom_call_target="tpu_custom_call" | custom-call | tf_op jit(solution)/shard_map/finish/pallas_call | solution.py:473
  176.1 1.3 dynamic-slice_bitcast_fusion
  177.3 1.6 copy.22
  178.9 1.6 copy.23
  180.5 4.1 %copy.24 = bf16[2,384,2048]{2,1,0:T(8,128)(2,1)} copy(bf16[2,384,2048]{2,1,0:T(8,128)(2,1)} %get-tuple-element.65) | data formatting | bytes 6291456
  184.6 1.7 copy.25
  186.2 1.4 copy-done.11
  187.6 1.7 copy.26
  (35 shorter events, 0.4 us)
Async XLA Ops:
  0.6 9.4 %copy-start = (bf16[2,384,2048]{2,1,0:T(8,128)(2,1)S(1)}, bf16[2,384,2048]{2,1,0:T(8,128)(2,1)}, u32[]{:S(2)}) copy-start(bf16[2,384,2048]{2,1,0:T(8,128)(2,1)} %wd_ref.1) | copy-start | bytes 9437188
  66.1 7.2 %copy-start.13 = (bf16[1024,2048]{1,0:T(8,128)(2,1)S(1)}, bf16[1024,2048]{1,0:T(8,128)(2,1)}, u32[]{:S(2)}) copy-start(bf16[1024,2048]{1,0:T(8,128)(2,1)} %get-tuple-element.17) | copy-start | bytes 12582916
  73.3 7.5 %copy-start.9 = (bf16[3,352,2048]{2,1,0:T(8,128)(2,1)}, bf16[3,352,2048]{2,1,0:T(8,128)(2,1)S(1)}, u32[]{:S(2)}) copy-start(bf16[3,352,2048]{2,1,0:T(8,128)(2,1)S(1)} %fusion.19.rin_ref) | copy-start | bytes 12976132
  73.3 5.0 %copy-start.1 = (bf16[2,384,2048]{2,1,0:T(8,128)(2,1)S(1)}, bf16[2,384,2048]{2,1,0:T(8,128)(2,1)}, u32[]{:S(2)}) copy-start(bf16[2,384,2048]{2,1,0:T(8,128)(2,1)} %wu_ref.1) | copy-start | bytes 9437188
  73.3 5.0 %copy-start.5 = (bf16[1,384,2048]{2,1,0:T(8,128)(2,1)S(1)}, bf16[1,384,2048]{2,1,0:T(8,128)(2,1)}, u32[]{:S(2)}) copy-start(bf16[1,384,2048]{2,1,0:T(8,128)(2,1)} %get-tuple-element.55.cu_ref) | copy-start | bytes 4718596
  78.4 6.3 %copy-start.10 = (bf16[3,352,2048]{2,1,0:T(8,128)(2,1)}, bf16[3,352,2048]{2,1,0:T(8,128)(2,1)S(1)}, u32[]{:S(2)}) copy-start(bf16[3,352,2048]{2,1,0:T(8,128)(2,1)S(1)} %fusion.22.rcot_ref) | copy-start | bytes 12976132
  78.4 3.5 %copy-start.2 = (bf16[2,384,2048]{2,1,0:T(8,128)(2,1)S(1)}, bf16[2,384,2048]{2,1,0:T(8,128)(2,1)}, u32[]{:S(2)}) copy-start(bf16[2,384,2048]{2,1,0:T(8,128)(2,1)} %wg_ref.1) | copy-start | bytes 9437188
  78.4 3.9 %copy-start.3 = (bf16[1,384,2048]{2,1,0:T(8,128)(2,1)S(1)}, bf16[1,384,2048]{2,1,0:T(8,128)(2,1)}, u32[]{:S(2)}) copy-start(bf16[1,384,2048]{2,1,0:T(8,128)(2,1)} %constant_dynamic-slice_fusion.2.cg_ref) | copy-start | bytes 4718596
  82.3 2.4 %copy-start.4 = (bf16[1,384,2048]{2,1,0:T(8,128)(2,1)S(1)}, bf16[1,384,2048]{2,1,0:T(8,128)(2,1)}, u32[]{:S(2)}) copy-start(bf16[1,384,2048]{2,1,0:T(8,128)(2,1)} %get-tuple-element.54.cd_ref) | copy-start | bytes 4718596
  89.7 2.6 %copy-start.6 = (bf16[3,352,384]{2,1,0:T(8,128)(2,1)}, bf16[3,352,384]{2,1,0:T(8,128)(2,1)S(1)}, u32[]{:S(2)}) copy-start(bf16[3,352,384]{2,1,0:T(8,128)(2,1)S(1)} %get-tuple-element.37.du_ref) | copy-start | bytes 2433028
  89.7 2.5 %copy-start.7 = (bf16[3,352,384]{2,1,0:T(8,128)(2,1)}, bf16[3,352,384]{2,1,0:T(8,128)(2,1)S(1)}, u32[]{:S(2)}) copy-start(bf16[3,352,384]{2,1,0:T(8,128)(2,1)S(1)} %get-tuple-element.38.dg_ref) | copy-start | bytes 2433028
  89.7 2.5 %copy-start.8 = (bf16[3,352,384]{2,1,0:T(8,128)(2,1)}, bf16[3,352,384]{2,1,0:T(8,128)(2,1)S(1)}, u32[]{:S(2)}) copy-start(bf16[3,352,384]{2,1,0:T(8,128)(2,1)S(1)} %get-tuple-element.39.hid_ref) | copy-start | bytes 2433028
  180.5 4.1 %copy-start.12 = (bf16[2,384,2048]{2,1,0:T(8,128)(2,1)S(1)}, bf16[2,384,2048]{2,1,0:T(8,128)(2,1)}, u32[]{:S(2)}) copy-start(bf16[2,384,2048]{2,1,0:T(8,128)(2,1)} %get-tuple-element.66) | copy-start | bytes 9437188
  184.6 3.0 %copy-start.11 = (bf16[2,384,2048]{2,1,0:T(8,128)(2,1)S(1)}, bf16[2,384,2048]{2,1,0:T(8,128)(2,1)}, u32[]{:S(2)}) copy-start(bf16[2,384,2048]{2,1,0:T(8,128)(2,1)} %get-tuple-element.67) | copy-start | bytes 9437188
where the time goes:
time: 192 us; the launch traced here: 189 us
  Pallas kernels  132 us (69%)
  local copies, waits for them, and re-layouts  22.3 us (12%)
  matrix products  19.6 us (10%)
  other arithmetic  10.9 us (6%)
  between operations  4.18 us (2%)
    pallas_call x1, Pallas kernels, finish(): pl.pallas_call(functools.partial(finish_kernel, sizes), out_shape=(block,...  80.9 us
    pallas_call x1, Pallas kernels, gather_all(): pl.pallas_call(functools.partial(gather_kernel, sizes), out_shape=(whole,...  51.4 us
    unnamed x33, local copies, waits for them, and re-layouts  13.5 us
    dot_general x1, matrix products, body(): jnp.einsum('crt,td->crd', pick, tok, preferred_element_type=f32)  7.18 us
    dynamic_slice x2, local copies, waits for them, and re-layouts, body(): lax.dynamic_index_in_dim(w, own_pick, 0, keepdims=True)  6.14 us
    dot_general x1, matrix products, body(): jnp.einsum('crt,td->crd', pick, cot, preferred_element_type=f32)  5.01 us

commit v1 on v0

--- a/solution.py
+++ b/solution.py
@@ -149,6 +149,145 @@
         ],
         compiler_params=pltpu.CompilerParams(collective_id=0, has_side_effects=True),
         name="gather_all",
+    )(tokens, cotangent, meta)
+
+
+def gather_rows_kernel(sizes, tok_ref, cot_ref, meta_ref, rin_ref, rcot_ref, meta_out, tok_out, cot_out, pick, picked, send, recv, own, stored):
+    place = Place(sizes)
+    rows, columns = tok_ref.shape
+
+    def view(a, ref, d):
+        if a == 2:
+            return ref.at[place.expert_of(d)]
+        return place.block(ref, d, rows, columns)
+
+    ins, outs = (tok_ref, cot_ref, meta_ref), (tok_out, cot_out, meta_out)
+    orders = GATHER_ORDERS + ((0, 1),)
+    zero = (0, 0, 0, 0)
+    local = [pltpu.make_async_copy(ins[a], view(a, outs[a], zero), own.at[a]) for a in range(3)]
+    for copy in local:
+        copy.start()
+    place.greet()
+    sent = []
+
+    def stage_of(a, d):
+        return max([p for p, dim in enumerate(orders[a]) if d[dim]], default=-1)
+
+    def forward(a, d, p):
+        for step in place.steps(orders[a][p]):
+            there = plus(d, step)
+            n = place.number(there)
+            src = ins[a] if d == zero else view(a, outs[a], d)
+            copy = remote(src, view(a, outs[a], d), send.at[a, n], recv.at[a, n], place.device(step))
+            copy.start()
+            sent.append(copy)
+
+    for p in range(4):
+        for a in (2, 0, 1):
+            if p < len(orders[a]):
+                forward(a, zero, p)
+    copies, slot_rows, total = pick.shape
+    groups, lines_of, tok_dev = meta_out.shape
+    half = sizes[0] * sizes[1] // 2
+    f32, bf16 = jnp.float32, jnp.bfloat16
+    stores = []
+
+    def build():
+        partner = lax.rem(place.expert + half, groups)
+        names = [place.expert * copies + c for c in range(copies - 1)] + [partner * copies + copies - 1]
+        earlier = lax.broadcasted_iota(jnp.int32, (tok_dev, tok_dev), 0)
+        later = lax.broadcasted_iota(jnp.int32, (tok_dev, tok_dev), 1)
+        tri = (earlier <= later).astype(f32).astype(bf16)
+        slot = lax.broadcasted_iota(jnp.int32, (slot_rows, tok_dev), 0).astype(f32)
+        for c in range(copies):
+            name = names[c].astype(f32)
+            before = jnp.zeros((1, 1), f32)
+            for g in range(groups):
+                hit = meta_out[g][: lines_of // 2] == name
+                member = jnp.sum(hit.astype(f32), axis=0, keepdims=True)
+                wide = jnp.broadcast_to(member, (16, tok_dev)).astype(bf16)
+                inside = jnp.dot(wide, tri, preferred_element_type=f32)[:1]
+                at = jnp.where(member > 0, inside + before - 1.0, -1.0)
+                pick[c, :, pl.ds(g * tok_dev, tok_dev)] = (slot == at).astype(f32).astype(bf16)
+                before = before + jnp.sum(member, axis=1, keepdims=True)
+
+    def choose(a, d):
+        cols = pl.ds(pl.multiple_of(place.dp_of(d) * columns, columns), columns)
+
+        @pl.loop(0, copies)
+        def _(c):
+            rows_of = jnp.dot(pick[c], outs[a][:, cols], preferred_element_type=f32)
+            picked[a, c, :, cols] = rows_of.astype(bf16)
+
+        target = (rin_ref, rcot_ref)[a]
+        copy = pltpu.make_async_copy(picked.at[a, :, :, cols], target.at[:, :, cols], stored.at[a, d[2] * 2 + d[3]])
+        copy.start()
+        stores.append(copy)
+
+    def take(a, d):
+        n = place.number(d)
+        here = view(a, outs[a], d)
+        remote(here, here, send.at[a, n], recv.at[a, n], place.device(place.steps(0)[0])).wait_recv()
+
+    for stage in range(3):
+        todo = []
+        for a in (2, 0, 1):
+            if stage < len(orders[a]):
+                mine = [d for d in place.ids if all(d[x] == 0 for x in range(4) if x not in orders[a])]
+                todo += [(i, a, d) for i, d in enumerate([d for d in mine if stage_of(a, d) == stage])]
+        for _, a, d in sorted(todo, key=lambda t: t[0]):
+            take(a, d)
+            for p in range(stage + 1, len(orders[a])):
+                forward(a, d, p)
+        if stage == 1:
+            for copy in local:
+                copy.wait()
+            build()
+            choose(0, zero)
+        if stage == 2:
+            choose(1, zero)
+            for dx in range(1, sizes[2]):
+                choose(0, (0, 0, dx, 0))
+                choose(1, (0, 0, dx, 0))
+    for dx in range(sizes[2]):
+        for a in range(2):
+            for d in place.ids:
+                if d[2:] == (dx, 1):
+                    take(a, d)
+            choose(a, (0, 0, dx, 1))
+    for copy in stores:
+        copy.wait()
+    for copy in sent:
+        copy.wait_send()
+
+
+def gather_rows(tokens, cotangent, meta, copies, slot_rows):
+    sizes = lines()
+    groups, dps = lax.axis_size("expert"), lax.axis_size("dp")
+    devices = groups * dps
+    total, features = groups * tokens.shape[0], dps * tokens.shape[1]
+    picked = (copies, slot_rows, features)
+    out = jax.ShapeDtypeStruct(picked, jnp.bfloat16)
+    anywhere = pl.BlockSpec(memory_space=pl.ANY)
+    return pl.pallas_call(
+        functools.partial(gather_rows_kernel, sizes),
+        out_shape=(out, out, jax.ShapeDtypeStruct((groups,) + meta.shape, meta.dtype)),
+        in_specs=[anywhere] * 3,
+        out_specs=[anywhere] * 2 + [pl.BlockSpec(memory_space=pltpu.VMEM)],
+        scratch_shapes=[
+            pltpu.VMEM((total, features), jnp.bfloat16),
+            pltpu.VMEM((total, features), jnp.bfloat16),
+            pltpu.VMEM((copies, slot_rows, total), jnp.bfloat16),
+            pltpu.VMEM((2,) + picked, jnp.bfloat16),
+            pltpu.SemaphoreType.DMA((3, devices)),
+            pltpu.SemaphoreType.DMA((3, devices)),
+            pltpu.SemaphoreType.DMA((3,)),
+            pltpu.SemaphoreType.DMA((2, dps)),
+        ],
+        compiler_params=pltpu.CompilerParams(
+            collective_id=0, has_side_effects=True, vmem_limit_bytes=40 * 1024 * 1024
+        ),
+        name="gather_rows",
     )(tokens, cotangent, meta)
 
 
@@ -513,7 +652,12 @@
     f32, bf16 = jnp.float32, jnp.bfloat16
 
     meta = jnp.concatenate([route.T.astype(f32), gate_prob.T], axis=0)
-    tok, cot, meta = gather_all(tokens, cotangent, meta)
+    fits = 8 * total * features <= 1 << 25
+    if fits:
+        rows_in, rows_cot, meta = gather_rows(tokens, cotangent, meta, local_copies, rows)
+    else:
+        tok, cot, meta = gather_all(tokens, cotangent, meta)
+    meta, replica_pick = lax.optimization_barrier((meta, replica_pick))
     meta = jnp.transpose(meta, (1, 0, 2)).reshape(2 * fanout, total)
     route_t = meta[:fanout].astype(jnp.int32)
     gate_t = meta[fanout:]
@@ -543,7 +687,9 @@
     up_w = jnp.concatenate([w_up, chosen[1]], axis=0)
     down_w = jnp.concatenate([w_down, chosen[2]], axis=0)
 
-    rows_in = jnp.einsum("crt,td->crd", pick, tok, preferred_element_type=f32).astype(bf16)
+    if not fits:
+        rows_in = jnp.einsum("crt,td->crd", pick, tok, preferred_element_type=f32).astype(bf16)
+        rows_cot = jnp.einsum("crt,td->crd", pick, cot, preferred_element_type=f32).astype(bf16)
     gate_act = jnp.einsum("crd,cfd->crf", rows_in, gate_w, preferred_element_type=f32)
     up_act = jnp.einsum("crd,cfd->crf", rows_in, up_w, preferred_element_type=f32)
     sig = jax.nn.sigmoid(gate_act)
@@ -552,7 +698,6 @@
     g = gate_rows[:, :, None]
     hidden_g = (g * hidden).astype(bf16)
 
-    rows_cot = jnp.einsum("crt,td->crd", pick, cot, preferred_element_type=f32).astype(bf16)
     back_h = jnp.einsum("crd,cfd->crf", rows_cot, down_w, preferred_element_type=f32)
     gg_rows = jnp.sum(hidden * back_h, axis=2)
     d_hidden = g * back_h
@@ -562,7 +707,7 @@
     gg = sum(jnp.where(h, gg_tok[j][None], 0.0) for j, h in enumerate(hits))
     gg = jnp.transpose(gg.reshape(fanout, groups, tok_dev), (1, 0, 2))
     share = fanout // lax.axis_size("dp")
-    if 8 * total * features > 1 << 25:
+    if not fits:
         out_rows = jnp.einsum("crf,cfd->crd", hidden_g, down_w, preferred_element_type=f32).astype(bf16)
         out_tok = jnp.einsum("crt,crd->td", pick, out_rows, preferred_element_type=f32).astype(bf16)
         back_rows = jnp.einsum("crf,cfd->crd", d_gate, gate_w, preferred_element_type=f32)

time: 192 us -> 190 us (0.990)
  matrix products: 19.6 us -> 10.7 us
  Pallas kernels: 132 us -> 139 us
    dot_general x2 -> x0, matrix products: 12.2 us -> none  [the longest x1 7.18 us: body(): jnp.einsum('crt,td->crd', pick, tok, preferred_element_type=f32)]
    pallas_call x1, Pallas kernels: 51.4 us -> 62 us  [gather_rows(): pl.pallas_call(functools.partial(gather_rows_kernel, sizes), out_shape=(o...]
    unnamed x33 -> x43, local copies, waits for them, and re-layouts: 13.5 us -> 18.6 us
    dynamic_slice x2, local copies, waits for them, and re-layouts: 6.14 us -> 2.24 us  [body(): lax.dynamic_index_in_dim(w, own_pick, 0, keepdims=True)]
    pallas_call x1, Pallas kernels: 80.9 us -> 77.2 us  [finish(): pl.pallas_call(functools.partial(finish_kernel, sizes), out_shape=(block,...]
    dot_general x1, matrix products: 2.4 us -> 5.57 us  [body(): jnp.einsum('crd,cfd->crf', rows_in, gate_w, preferred_element_type=f32)]
where the time goes in v1:
time: 190 us; the launch traced here: 187 us
  Pallas kernels  139 us (73%)
  local copies, waits for them, and re-layouts  23.3 us (12%)
  matrix products  10.7 us (6%)
  other arithmetic  9.56 us (5%)
  between operations  4.22 us (2%)
    pallas_call x1, Pallas kernels, finish(): pl.pallas_call(functools.partial(finish_kernel, sizes), out_shape=(block,...  77.2 us
    pallas_call x1, Pallas kernels, gather_rows(): pl.pallas_call(functools.partial(gather_rows_kernel, sizes), out_shape=(o...  62 us
    unnamed x43, local copies, waits for them, and re-layouts  18.6 us
    dot_general x1, matrix products, body(): jnp.einsum('crd,cfd->crf', rows_in, gate_w, preferred_element_type=f32)  5.57 us

profile of v1, /device:TPU:0, one launch (start us, length us, event | category | flops | bytes accessed | tf_op | source)
XLA Modules:
  0.0 187.0 jit_solution(5385925570822820816)
XLA Ops:
  0.7 0.7 convert_bitcast_fusion
  1.4 0.7 pad_maximum_fusion.3.meta_ref
  2.1 0.9 copy-done.2
  3.0 0.9 copy-done.3
  3.9 62.0 %gather_rows.1 = (bf16[3,352,2048]{2,1,0:T(8,128)(2,1)S(1)}, bf16[3,352,2048]{2,1,0:T(8,128)(2,1)S(1)}, f32[8,16,128]{2,1,0:T(8,128)S(1)}) custom-call(bf16[128,512]{1,0:T(8,128)(2,1)S(1)} %copy-done.2, bf16[128,512]{1,0:T(8,128)(2,1)S(1)} %copy-done.3, f32[16,128]{1,0:T(8,128)S(1)} %pad_maximum_fusion.3.meta_ref), custom_call_target="tpu_custom_call" | custom-call | tf_op jit(solution)/shard_map/gather_rows/pallas_call | solution.py:272
  65.9 2.0 %copy-done = bf16[3,352,2048]{2,1,0:T(8,128)(2,1)} copy-done((bf16[3,352,2048]{2,1,0:T(8,128)(2,1)}, bf16[3,352,2048]{2,1,0:T(8,128)(2,1)S(1)}, u32[]{:S(2)}) %copy-start) | copy-done | bytes 4325400
  67.8 2.0 %copy-done.1 = bf16[3,352,2048]{2,1,0:T(8,128)(2,1)} copy-done((bf16[3,352,2048]{2,1,0:T(8,128)(2,1)}, bf16[3,352,2048]{2,1,0:T(8,128)(2,1)S(1)}, u32[]{:S(2)}) %copy-start.1) | copy-done | bytes 4325400
  69.9 1.2 dynamic_slice.16
  74.5 0.1 multiply_reduce_fusion.1
  74.6 0.1 fusion.19
  74.7 0.1 select_bitcast_fusion
  74.9 1.8 constant_dynamic-slice_fusion.2.cg_ref
  76.8 5.6 %fusion = f32[3,352,384]{2,1,0:T(8,128)S(1)} fusion(bf16[3,352,2048]{2,1,0:T(8,128)(2,1)} %copy-done, bf16[1,384,2048]{2,1,0:T(8,128)(2,1)S(1)} %constant_dynamic-slice_fusion.2.cg_ref, bf16[2,384,2048]{2,1,0:T(8,128)(2,1)S(1)} %copy-done.6), kind=kOutput, calls=%fused_computation | convolution fusion | flops 1663303680 | bytes 10665984 | tf_op jit(solution)/shard_map/crd,cfd->crf/dot_general | solution.py:693
  82.4 2.9 %fusion.15.pt_ref = bf16[1024,1056]{1,0:T(8,128)(2,1)} fusion(s32[1024]{0:T(1024)S(1)} %bitcast.60, s32[1024]{0:T(1024)S(1)} %bitcast.61, s32[1024]{0:T(1024)S(1)} %bitcast.59), kind=kLoop, calls=%fused_computation.21 | loop fusion | flops 12976128 | bytes 2174976 | tf_op jit(solution)/shard_map/add | solution.py:730
  85.3 0.4 constant_dynamic-slice_fusion
  85.7 2.4 %fusion.4 = f32[3,352,384]{2,1,0:T(8,128)S(1)} fusion(bf16[3,352,2048]{2,1,0:T(8,128)(2,1)S(1)} %bitcast.46, bf16[1,384,2048]{2,1,0:T(8,128)(2,1)S(1)} %get-tuple-element.59.cu_ref, bf16[2,384,2048]{2,1,0:T(8,128)(2,1)S(1)} %copy-done.5), kind=kOutput, calls=%fused_computation.4 | convolution fusion | flops 1663303680 | bytes 10665984 | tf_op jit(solution)/shard_map/crd,cfd->crf/dot_general | solution.py:694
  88.2 0.4 slice-done.2
  88.6 2.7 %multiply_reduce_fusion = (f32[3,352]{1,0:T(4,128)S(1)}, f32[3,352,384]{2,1,0:T(8,128)S(1)}) fusion(f32[3,352,384]{2,1,0:T(8,128)S(1)} %fusion.4, f32[3,352,384]{2,1,0:T(8,128)S(1)} %fusion, bf16[3,352,2048]{2,1,0:T(8,128)(2,1)S(1)} %bitcast.48, bf16[1,384,2048]{2,1,0:T(8,128)(2,1)S(1)} %get-tuple-element.58.cd_ref, bf16[2,384,2048]{2,1,0:T(8,128)(2,1)S(1)} %copy-done.4), kind=kOutput, calls=%fused_computation.24 | convolution fusion | flops 1666141184 | bytes 13914240 | tf_op jit(solution)/shard_map/crd,cfd->crf/dot_general | solution.py:701
  91.3 1.4 select_reduce_fusion
  92.7 1.1 multiply_convert_fusion
  93.8 0.7 add_bitcast_fusion.gg_ref
  94.8 0.1 copy-done.11
  95.0 0.2 copy-done.12
  95.2 1.4 pad_maximum_fusion.sel_ref
  96.6 77.2 %finish.1 = (bf16[128,512]{1,0:T(8,128)(2,1)}, bf16[128,512]{1,0:T(8,128)(2,1)}, f32[8,128]{1,0:T(8,128)}, bf16[2,384,2048]{2,1,0:T(8,128)(2,1)}, bf16[2,384,204...) custom-call(bf16[3,352,384]{2,1,0:T(8,128)(2,1)} %copy-done.12, bf16[3,352,384]{2,1,0:T(8,128)(2,1)} %copy-done.11, ...), custom_call_target="tpu_custom_call" | custom-call | tf_op jit(solution)/shard_map/finish/pallas_call | solution.py:612
  173.8 1.3 dynamic-slice_bitcast_fusion
  175.0 1.6 copy.22
  176.6 1.6 copy.23
  178.1 4.1 %copy.24 = bf16[2,384,2048]{2,1,0:T(8,128)(2,1)} copy(bf16[2,384,2048]{2,1,0:T(8,128)(2,1)} %get-tuple-element.69) | data formatting | bytes 6291456
  182.3 1.7 copy.25
  183.9 1.4 copy-done.13
  185.3 1.7 copy.26
  (45 shorter events, 0.6 us)
Async XLA Ops:
  2.1 0.9 copy-start.2
  3.0 0.9 copy-start.3
  65.8 2.0 %copy-start = (bf16[3,352,2048]{2,1,0:T(8,128)(2,1)}, bf16[3,352,2048]{2,1,0:T(8,128)(2,1)S(1)}, u32[]{:S(2)}) copy-start(bf16[3,352,2048]{2,1,0:T(8,128)(2,1)S(1)} %get-tuple-element.19.rin_ref) | copy-start | bytes 12976132
  67.8 2.0 %copy-start.1 = (bf16[3,352,2048]{2,1,0:T(8,128)(2,1)}, bf16[3,352,2048]{2,1,0:T(8,128)(2,1)S(1)}, u32[]{:S(2)}) copy-start(bf16[3,352,2048]{2,1,0:T(8,128)(2,1)S(1)} %get-tuple-element.21.rcot_ref) | copy-start | bytes 12976132
  74.4 2.4 %copy-start.6 = (bf16[2,384,2048]{2,1,0:T(8,128)(2,1)S(1)}, bf16[2,384,2048]{2,1,0:T(8,128)(2,1)}, u32[]{:S(2)}) copy-start(bf16[2,384,2048]{2,1,0:T(8,128)(2,1)} %wg_ref.1) | copy-start | bytes 9437188
  74.9 10.8 %slice-start = ((s8[4325376]{0:T(1024)(128)(4,1)}), s8[4194304]{0:T(1024)(128)(4,1)S(1)}, s32[]{:S(2)}) async-start(s8[4325376]{0:T(1024)(128)(4,1)} %bitcast.45), calls=%async_computation | async-start | bytes 8388608
  76.7 5.6 %copy-start.7 = (bf16[1,384,2048]{2,1,0:T(8,128)(2,1)}, bf16[1,384,2048]{2,1,0:T(8,128)(2,1)S(1)}, u32[]{:S(2)}) copy-start(bf16[1,384,2048]{2,1,0:T(8,128)(2,1)S(1)} %constant_dynamic-slice_fusion.2.cg_ref) | copy-start | bytes 4718596
  76.8 8.5 %copy-start.4 = (bf16[2,384,2048]{2,1,0:T(8,128)(2,1)S(1)}, bf16[2,384,2048]{2,1,0:T(8,128)(2,1)}, u32[]{:S(2)}) copy-start(bf16[2,384,2048]{2,1,0:T(8,128)(2,1)} %wd_ref.1) | copy-start | bytes 9437188
  76.8 8.5 %copy-start.5 = (bf16[2,384,2048]{2,1,0:T(8,128)(2,1)S(1)}, bf16[2,384,2048]{2,1,0:T(8,128)(2,1)}, u32[]{:S(2)}) copy-start(bf16[2,384,2048]{2,1,0:T(8,128)(2,1)} %wu_ref.1) | copy-start | bytes 9437188
  76.8 8.9 %slice-start.1 = ((s8[4325376]{0:T(1024)(128)(4,1)}), s8[131072]{0:T(1024)(128)(4,1)S(1)}, s32[]{:S(2)}) async-start(s8[4325376]{0:T(1024)(128)(4,1)} %bitcast.45), calls=%async_computation.1 | async-start | bytes 262144
  85.3 3.3 %slice-start.2 = ((s8[4325376]{0:T(1024)(128)(4,1)}), s8[4194304]{0:T(1024)(128)(4,1)S(1)}, s32[]{:S(2)}) async-start(s8[4325376]{0:T(1024)(128)(4,1)} %bitcast.47), calls=%async_computation.2 | async-start | bytes 8388608
  85.7 2.5 %copy-start.8 = (bf16[1,384,2048]{2,1,0:T(8,128)(2,1)}, bf16[1,384,2048]{2,1,0:T(8,128)(2,1)S(1)}, u32[]{:S(2)}) copy-start(bf16[1,384,2048]{2,1,0:T(8,128)(2,1)S(1)} %get-tuple-element.58.cd_ref) | copy-start | bytes 4718596
  85.7 2.5 %copy-start.9 = (bf16[1,384,2048]{2,1,0:T(8,128)(2,1)}, bf16[1,384,2048]{2,1,0:T(8,128)(2,1)S(1)}, u32[]{:S(2)}) copy-start(bf16[1,384,2048]{2,1,0:T(8,128)(2,1)S(1)} %get-tuple-element.59.cu_ref) | copy-start | bytes 4718596
  85.7 2.9 %slice-start.3 = ((s8[4325376]{0:T(1024)(128)(4,1)}), s8[131072]{0:T(1024)(128)(4,1)S(1)}, s32[]{:S(2)}) async-start(s8[4325376]{0:T(1024)(128)(4,1)} %bitcast.47), calls=%async_computation.3 | async-start | bytes 262144
  93.7 1.1 copy-start.10
  93.7 1.2 copy-start.11
  93.7 1.4 copy-start.12
  178.1 4.1 %copy-start.14 = (bf16[2,384,2048]{2,1,0:T(8,128)(2,1)S(1)}, bf16[2,384,2048]{2,1,0:T(8,128)(2,1)}, u32[]{:S(2)}) copy-start(bf16[2,384,2048]{2,1,0:T(8,128)(2,1)} %get-tuple-element.70) | copy-start | bytes 9437188
  182.3 3.0 %copy-start.13 = (bf16[2,384,2048]{2,1,0:T(8,128)(2,1)S(1)}, bf16[2,384,2048]{2,1,0:T(8,128)(2,1)}, u32[]{:S(2)}) copy-start(bf16[2,384,2048]{2,1,0:T(8,128)(2,1)} %get-tuple-element.71) | copy-start | bytes 9437188
